TPU v7x, 32 devices: a whole 2x2x4 slice. The times are simulated.
32 devices in a mesh: ctx: 8 (over y, x, core), mp: 4 (over z).
Axes of the slice: x: 2, y: 2, z: 4, core: 2. Of those that a mesh axis runs over, the one named last changes fastest.
Arguments:
- source_rows: bfloat16 [4096, 3, 8192], P('ctx', None, 'mp'), may hold values from -6 to 6
- short_filters: bfloat16 [3, 7, 8192], P(None, None, 'mp'), may hold values from -2 to 2
- medium_filters: bfloat16 [128, 512], P(None, 'mp'), may hold values from -0.5 to 0.5
- skip_gain: float32 [8192], P('mp'), may hold values from 0.1 to 1.9
- out_weight: bfloat16 [8192, 8192], P('mp', 'ctx'), may hold values from -0.0625 to 0.0625
- doc_lengths: int32 [8], replicated, may hold values from 1 to 512, 2048 in all
- block_packing_device: int32 [8, 4], replicated, may hold values from 0 to 7, as said below
Outputs:
- mixed: bfloat16 [2048, 8192], P('ctx', 'mp')
Inputs may be any that keep to these rules, and one draw needn't show every extreme that they name: `block_packing_device`: row c names, for the 4 blocks of stretch c in order, the packing device that holds each; the entries of one row differ, and some packing device is named in every row. A packing device keeps the blocks it holds in increasing order of their stretch, in its first slots.
All inputs are finite; a program needn't handle non-finite values.
Results may differ from a plain program's by a relative error of at most 0.02.
Values may be sent and summed in bfloat16 or wider, within the bound.
A program may use at most 192 MiB of HBM per device.

v0:
```python
import jax
import jax.numpy as jnp
from jax import lax
from jax.sharding import PartitionSpec as P


def passed_along(block, axis, distance):
    devices = range(lax.axis_size(axis))
    route = [(i - distance, i) for i in devices if i - distance in devices]
    return lax.ppermute(block, axis, route)


def reach_back(positions, starts):
    begin = jnp.max(jnp.where(starts[None, :] <= positions[:, None], starts[None, :], 0), axis=1)
    return positions - begin


def short_conv(extended, filt, back, count):
    span = filt.shape[0]
    taps = filt.astype(jnp.float32)
    total = jnp.zeros((count, extended.shape[1]), jnp.float32)
    for step in range(span):
        keep = (back >= step).astype(jnp.float32)[:, None]
        piece = extended[span - 1 - step : span - 1 - step + count].astype(jnp.float32)
        total = total + taps[step][None, :] * piece * keep
    return total


def on_device(
    source_rows,
    short_filters,
    medium_filters,
    skip_gain,
    out_weight,
    doc_lengths,
    block_packing_device,
):
    stretches = lax.axis_size("ctx")
    rank_me = lax.axis_index("ctx")
    nb_own = block_packing_device.shape[1]
    blk = source_rows.shape[0] // stretches
    rows = nb_own * blk
    width = source_rows.shape[2]
    se_len = short_filters.shape[1]
    mr_len = medium_filters.shape[0]
    member = jnp.any(block_packing_device == rank_me, axis=1)
    flags = member.astype(jnp.int32)
    slots = jnp.cumsum(flags) - flags
    blocks = source_rows.reshape(stretches, blk, 3, width)
    outgoing = jnp.where(
        member[:, None, None, None], jnp.take(blocks, slots, axis=0), jnp.zeros((), jnp.bfloat16)
    )
    incoming = lax.all_to_all(outgoing, "ctx", split_axis=0, concat_axis=0, tiled=True)
    wanted = lax.dynamic_index_in_dim(block_packing_device, rank_me, 0, keepdims=False)
    stretch = jnp.take(incoming, wanted, axis=0).reshape(rows, 3, width)
    ends = jnp.cumsum(doc_lengths)
    starts = ends - doc_lengths
    base = rank_me * rows
    positions = base + jnp.arange(rows, dtype=jnp.int32)
    back = reach_back(positions, starts)
    span_cols = rows + mr_len - 1
    edge = stretch[rows - (se_len - 1) :]
    earlier = passed_along(edge, "ctx", 1)
    extended = jnp.concatenate([earlier, stretch], axis=0)
    query = short_conv(extended[:, 0], short_filters[0], back, rows)
    keyed = short_conv(extended[:, 1], short_filters[1], back, rows)
    valued = short_conv(extended[:, 2], short_filters[2], back, rows)
    z_vals = (keyed * valued).astype(jnp.bfloat16)
    z_prev = passed_along(z_vals[rows - (mr_len - 1) :], "ctx", 1)
    z_ext = jnp.concatenate([z_prev, z_vals], axis=0)
    groups_dev = medium_filters.shape[1]
    per_group = width // groups_dev
    reversed_taps = jnp.transpose(medium_filters[::-1])
    line = jnp.concatenate([reversed_taps, jnp.zeros((groups_dev, rows), jnp.bfloat16)], axis=1)
    band = jnp.tile(line, (1, rows + 1))[:, : rows * span_cols].reshape(groups_dev, rows, span_cols)
    ext_pos = base - (mr_len - 1) + jnp.arange(span_cols, dtype=jnp.int32)
    begin_rows = positions - back
    keep = ext_pos[None, :] >= begin_rows[:, None]
    band = jnp.where(keep[None, :, :], band, jnp.zeros((), jnp.bfloat16))
    medium = jnp.einsum(
        "gip,pgc->igc",
        band,
        z_ext.reshape(span_cols, groups_dev, per_group),
        preferred_element_type=jnp.float32,
    ).reshape(rows, width)
    hidden = (query * (medium + skip_gain[None, :] * z_vals.astype(jnp.float32))).astype(
        jnp.bfloat16
    )
    partial_value = jnp.dot(
        hidden,
        lax.all_gather(out_weight, "ctx", axis=1, tiled=True),
        preferred_element_type=jnp.float32,
    )
    return lax.psum_scatter(
        partial_value.astype(jnp.bfloat16), "mp", scatter_dimension=1, tiled=True
    )


def solution(mesh):
    return jax.shard_map(
        on_device,
        mesh=mesh,
        in_specs=(
            P("ctx", None, "mp"),
            P(None, None, "mp"),
            P(None, "mp"),
            P("mp"),
            P("mp", "ctx"),
            P(),
            P(),
        ),
        out_specs=P("ctx", "mp"),
        check_vma=False,
    )
```

profile of v0, /device:TPU:13, one launch (start us, length us, event | category | flops | bytes accessed | tf_op | source)
XLA Modules:
  0.0 371.6 jit_solution(12202680698718344489)
XLA Ops:
  6.5 0.7 all-gather.2.cloned.1.call-update
  7.3 0.2 reduce-window.14
  7.5 6.3 %gather_fusion = bf16[8,64,3,2048]{3,1,2,0:T(8,128)(2,1)} fusion(bf16[8,64,3,2048]{3,1,0,2:T(8,128)(2,1)} %bitcast.164, s32[1024]{0:T(1024)S(1)} %pad_clamp_fusion.1), kind=kCustom, calls=%fused_computation | custom fusion | bytes 12582944 | tf_op jit(solution)/shard_map/jit(_take)/gather | solution.py:51
  13.8 7.3 %select_select_fusion = bf16[8,64,3,2048]{3,1,2,0:T(8,128)(2,1)} fusion(bf16[8,64,3,2048]{3,1,2,0:T(8,128)(2,1)} %gather_fusion, pred[8]{0:T(512)(128)(4,1)S(1)} %compare_and_fusion, pred[8]{0:T(512)(128)(4,1)S(1)} %compare_reduce_fusion), kind=kLoop, calls=%fused_computation.24 | loop fusion | flops 6291456 | bytes 12582928 | tf_op jit(solution)/shard_map/jit(_where)/select_n | solution.py:50
  21.1 5.7 %all-to-all-start = ((bf16[8,64,3,2048]{3,1,2,0:T(8,128)(2,1)}), bf16[8,64,3,2048]{3,1,2,0:T(8,128)(2,1)}, u32[]{:S(2)}, u32[]{:S(2)}) async-start(bf16[8,64,3,2048]{3,1,2,0:T(8,128)(2,1)} %select_select_fusion), calls=%async_computation | async-start | bytes 12582912 | tf_op jit(solution)/shard_map/all_to_all | solution.py:53
  26.8 0.2 dynamic-slice_reduce_fusion
  27.0 0.1 broadcast_in_dim.54
  27.1 0.1 broadcast_in_dim.55
  27.2 0.2 reduce-window.15
  27.4 0.1 select_reduce_fusion
  27.6 0.1 fusion.110
  27.7 107.6 %all-to-all-done = bf16[8,64,3,2048]{3,1,2,0:T(8,128)(2,1)} async-done(((bf16[8,64,3,2048]{3,1,2,0:T(8,128)(2,1)}), bf16[8,64,3,2048]{3,1,2,0:T(8,128)(2,1)}, u32[]{:S(2)}, u32[]{:S(2)}) %all-to-all-start) | async-done | bytes 6291488 | tf_op jit(solution)/shard_map/all_to_all | solution.py:53
  135.2 3.5 gather_fusion.1
  138.8 0.2 copy.17
  139.0 0.5 bitcast_select_fusion
  139.6 4.6 %collective-permute-start = (bf16[6,3,2048]{2,0,1:T(8,128)(2,1)S(1)}, bf16[6,3,2048]{2,0,1:T(8,128)(2,1)S(1)}, u32[]{:S(2)}, u32[]{:S(2)}) collective-permute-start(bf16[6,3,2048]{2,0,1:T(8,128)(2,1)S(1)} %slice.268), channel_id=1, source_target_pairs={{0,4},{4,8},{8,12},{12,16},{16,20},{20,24},{24,28},{1,5},{5,9},{9,... | collective-permute-start | bytes 221192 | tf_op jit(solution)/shard_map/ppermute | solution.py:10
  144.2 3.4 collective-permute-done
  147.5 5.5 %fusion.7 = bf16[256,2048]{1,0:T(8,128)(2,1)S(1)} fusion(bf16[6,3,2048]{2,0,1:T(8,128)(2,1)S(1)} %collective-permute-done, bf16[256,3,2048]{2,0,1:T(8,128)(2,1)S(1)} %bitcast_select_fusion, f32[2048]{0:T(1024)S(1)} %bitcast.169, f32[2048]{0:T(1024)S(1)} %bitcast.170, f32[2048]{0:T(1024)S(1)} %bitcast.171, f32[2048]{0:T(1024)S(1)} %bitcast.172, ...), kind=kLoop, calls=%fused_computation.30 | loop fusion | flops 54525952 | bytes 6511616 | tf_op jit(solution)/shard_map/convert_element_type | solution.py:68
  153.1 1.0 copy-done
  154.0 0.9 slice.324
  155.0 4.4 %collective-permute-start.1 = (bf16[127,2048]{1,0:T(8,128)(2,1)}, bf16[127,2048]{1,0:T(8,128)(2,1)}, u32[]{:S(2)}, u32[]{:S(2)}) collective-permute-start(bf16[127,2048]{1,0:T(8,128)(2,1)} %slice.324), channel_id=1, source_target_pairs={{0,4},{4,8},{8,12},{12,16},{16,20},{20,24},{24,28},{1,5},{5,9},{9,... | collective-permute-start | bytes 1560584 | tf_op jit(solution)/shard_map/ppermute | solution.py:10
  159.4 6.4 %tile.4 = bf16[128,257,384]{0,2,1:T(8,128)(2,1)S(1)} broadcast(bf16[128,384]{0,1:T(8,128)(2,1)S(1)} %concatenate.11), dimensions={0,2} | broadcast | bytes 25362432 | tf_op jit(solution)/shard_map/tile | solution.py:75
  165.9 9.5 %slice.325 = bf16[128,98048]{0,1:T(8,128)(2,1)} slice(bf16[128,98688]{0,1:T(8,128)(2,1)S(1)} %bitcast.163), slice={[0:128], [0:98048]} | slice | bytes 50200576 | tf_op jit(solution)/shard_map/slice | solution.py:75
  175.4 32.2 %reshape.350 = bf16[128,256,383]{0,2,1:T(8,128)(2,1)} reshape(bf16[128,98048]{0,1:T(8,128)(2,1)} %slice.325) | data formatting | bytes 50200576 | tf_op jit(solution)/shard_map/reshape | solution.py:75
  207.5 32.2 %copy.21 = bf16[128,256,383]{2,1,0:T(8,128)(2,1)} copy(bf16[128,256,383]{0,2,1:T(8,128)(2,1)} %reshape.350) | data formatting | bytes 50200576 | tf_op jit(solution)/shard_map/reshape | solution.py:75
  239.7 0.1 broadcast_compare_fusion
  239.9 2.8 pad_maximum_fusion
  242.7 2.6 copy.18
  245.2 13.0 %fusion = f32[128,16,256]{2,1,0:T(8,128)} fusion(bf16[383,128,16]{0,2,1:T(8,128)(2,1)} %bitcast.166, bf16[128,256,383]{2,1,0:T(8,128)(2,1)} %copy.21, pred[256,383]{1,0:T(8,128)(4,1)S(1)} %broadcast_compare_fusion), kind=kOutput, calls=%fused_computation.2 | convolution fusion | flops 414154752 | bytes 28864256 | tf_op jit(solution)/shard_map/gip,pgc->igc/dot_general | solution.py:80
  258.3 2.9 copy.20
  261.2 25.0 %convolution_convert_fusion = bf16[256,8192]{1,0:T(8,128)(2,1)} fusion(bf16[2048,8192]{1,0:T(8,128)(2,1)} %all-gather.2.cloned.1.call-done, f32[256,2048]{1,0:T(8,128)} %copy.20, bf16[256,2048]{1,0:T(8,128)(2,1)} %copy-done, bf16[6,3,2048]{2,0,1:T(8,128)(2,1)S(1)} %collective-permute-done, bf16[256,3,2048]{2,0,1:T(8,128)(2,1)S(1)} %bitcast_select_fusion, ...), kind=kOutput, calls=%fused_computation.23 | convolution fusion | flops 8621391872 | bytes 45259776 | tf_op jit(solution)/shard_map/dot_general | solution.py:89
  286.2 78.5 %reduce-scatter.2.cloned.1.call-done = bf16[256,2048]{1,0:T(8,128)(2,1)} async-done(((bf16[256,8192]{1,0:T(8,128)(2,1)}), bf16[256,2048]{1,0:T(8,128)(2,1)}) %reduce-scatter.2.cloned.1.call-update) | async-done | bytes 1048592 | tf_op jit(solution)/shard_map/reduce_scatter | solution.py:94
  (34 shorter events, 0.3 us)
Async XLA Ops:
  6.5 0.7 copy-start.3
  6.5 254.6 %all-gather.2.cloned.1.call-start = ((), (), s32[]{:S(2)}) async-start(), calls=%async_computation.2 | async-start | bytes 37748736 | tf_op jit(solution)/shard_map/all_gather | solution.py:91
  21.1 6.1 %copy-start.5 = (s32[8]{0:T(128)S(1)}, s32[8]{0:T(128)}, u32[]{:S(2)}) copy-start(s32[8]{0:T(128)} %param.12) | copy-start | bytes 100
  21.1 6.4 %copy-start.1 = (bf16[3,7,2048]{2,1,0:T(8,128)(2,1)S(1)}, bf16[3,7,2048]{2,1,0:T(8,128)(2,1)}, u32[]{:S(2)}) copy-start(bf16[3,7,2048]{2,1,0:T(8,128)(2,1)} %param.8) | copy-start | bytes 258052
  21.1 114.1 %all-to-all-start = ((bf16[8,64,3,2048]{3,1,2,0:T(8,128)(2,1)}), bf16[8,64,3,2048]{3,1,2,0:T(8,128)(2,1)}, u32[]{:S(2)}, u32[]{:S(2)}) async-start(bf16[8,64,3,2048]{3,1,2,0:T(8,128)(2,1)} %select_select_fusion), calls=%async_computation | async-start | bytes 12582912 | tf_op jit(solution)/shard_map/all_to_all | solution.py:53
  26.8 337.9 %reduce-scatter.2.cloned.1.call-start = ((), (), s32[]{:S(2)}) async-start(), calls=%async_computation.3 | async-start | bytes 5242880 | tf_op jit(solution)/shard_map/reduce_scatter | solution.py:94
  139.6 8.0 %collective-permute-start = (bf16[6,3,2048]{2,0,1:T(8,128)(2,1)S(1)}, bf16[6,3,2048]{2,0,1:T(8,128)(2,1)S(1)}, u32[]{:S(2)}, u32[]{:S(2)}) collective-permute-start(bf16[6,3,2048]{2,0,1:T(8,128)(2,1)S(1)} %slice.268), channel_id=1, source_target_pairs={{0,4},{4,8},{8,12},{12,16},{16,20},{20,24},{24,28},{1,5},{5,9},{9,... | collective-permute-start | bytes 221192 | tf_op jit(solution)/shard_map/ppermute | solution.py:10
  147.5 11.8 %copy-start.2 = (bf16[128,128]{1,0:T(8,128)(2,1)S(1)}, bf16[128,128]{1,0:T(8,128)(2,1)}, u32[]{:S(2)}) copy-start(bf16[128,128]{1,0:T(8,128)(2,1)} %param.9) | copy-start | bytes 98308
  153.0 1.0 copy-start
  155.0 84.9 %collective-permute-start.1 = (bf16[127,2048]{1,0:T(8,128)(2,1)}, bf16[127,2048]{1,0:T(8,128)(2,1)}, u32[]{:S(2)}, u32[]{:S(2)}) collective-permute-start(bf16[127,2048]{1,0:T(8,128)(2,1)} %slice.324), channel_id=1, source_target_pairs={{0,4},{4,8},{8,12},{12,16},{16,20},{20,24},{24,28},{1,5},{5,9},{9,... | collective-permute-start | bytes 1560584 | tf_op jit(solution)/shard_map/ppermute | solution.py:10
  258.3 2.9 copy-start.4
Sparse Core Ops, SparseCore 0:
  9.3 235.4 all-gather.1
  286.3 78.3 reduce-scatter.1
where the time goes:
time: 375 us; the launch traced here: 372 us
  waiting for transfers between devices  190 us (51%)
  local copies, waits for them, and re-layouts  98.3 us (26%)
  matrix products  38.1 us (10%)
  other arithmetic  16.8 us (4%)
  starting transfers between devices  14.7 us (4%)
  between operations  13.6 us (4%)
    all_to_all x1, waiting for transfers between devices, on_device(): lax.all_to_all(outgoing, 'ctx', split_axis=0, concat_axis=0, tiled=True)  108 us
    reduce_scatter x1, waiting for transfers between devices, on_device(): lax.psum_scatter(partial_value.astype(jnp.bfloat16), 'mp', scatter_dimens...  78.5 us
    reshape x2, local copies, waits for them, and re-layouts, on_device(): jnp.tile(line, (1, rows + 1))[:, :rows * span_cols]  64.4 us
    dot_general x1, matrix products, on_device(): jnp.dot(hidden, lax.all_gather(out_weight, 'ctx', axis=1, tiled=True), pr...  25 us
    dot_general x1, matrix products, on_device(): jnp.einsum('gip,pgc->igc', band, z_ext.reshape(span_cols, groups_dev, per...  13 us
    slice x1, local copies, waits for them, and re-layouts, on_device(): jnp.tile(line, (1, rows + 1))[:, :rows * span_cols]  9.5 us
    ppermute x2, starting transfers between devices, passed_along(): return lax.ppermute(block, axis, route)  8.95 us
  transfers between devices with their start and end apart: 5, of which 3 were waited for; matrix products, arithmetic and copies ran while one was open for 34% of the time, Pallas kernels for 0%

commit v1 on v0

v1 whole, which is shorter than its diff:
```python
import functools

import jax
import jax.numpy as jnp
from jax import lax
from jax.experimental import pallas as pl
from jax.experimental.pallas import tpu as pltpu
from jax.sharding import PartitionSpec as P

MESH = pl.DeviceIdType.MESH
EDGE = 16


def flipped(index, distance):
    bit = 1
    while bit <= distance:
        if distance & bit:
            index = index + bit * (1 - 2 * (lax.div(index, bit) % 2))
        bit *= 2
    return index


def passed_along(block, axis, distance):
    devices = range(lax.axis_size(axis))
    route = [(i - distance, i) for i in devices if i - distance in devices]
    return lax.ppermute(block, axis, route)


def exchange_kernel(n, out_ref, in_ref, send_sem, recv_sem, own_sem):
    me = lax.axis_index("ctx")
    mp = lax.axis_index("mp")
    barrier = pltpu.get_barrier_semaphore()
    for d in range(1, n):
        pl.semaphore_signal(barrier, inc=1, device_id=(flipped(me, d), mp), device_id_type=MESH)
    pl.semaphore_wait(barrier, n - 1)
    copies = []
    for d in reversed(range(1, n)):
        peer = flipped(me, d)
        copy = pltpu.make_async_remote_copy(
            src_ref=out_ref.at[peer],
            dst_ref=in_ref.at[me],
            send_sem=send_sem.at[d],
            recv_sem=recv_sem.at[d],
            device_id=(peer, mp),
            device_id_type=MESH,
        )
        copy.start()
        copies.append(copy)
    own = pltpu.make_async_copy(out_ref.at[me], in_ref.at[me], own_sem)
    own.start()
    own.wait()
    for d in range(1, n):
        peer = flipped(me, d)
        pltpu.make_async_remote_copy(
            src_ref=out_ref.at[peer],
            dst_ref=in_ref.at[peer],
            send_sem=send_sem.at[d],
            recv_sem=recv_sem.at[d],
            device_id=(peer, mp),
            device_id_type=MESH,
        ).wait()


def exchange(outgoing):
    n = outgoing.shape[0]
    return pl.pallas_call(
        functools.partial(exchange_kernel, n),
        out_shape=jax.ShapeDtypeStruct(outgoing.shape, outgoing.dtype),
        in_specs=[pl.BlockSpec(memory_space=pl.ANY)],
        out_specs=pl.BlockSpec(memory_space=pl.ANY),
        scratch_shapes=[
            pltpu.SemaphoreType.DMA((n,)),
            pltpu.SemaphoreType.DMA((n,)),
            pltpu.SemaphoreType.DMA,
        ],
        compiler_params=pltpu.CompilerParams(collective_id=0, has_side_effects=True),
        name="exchange",
    )(outgoing)


def short_kernel(nb, wanted_ref, *refs):
    block_refs = refs[:nb]
    edge_ref, filt_ref, back_ref, q_ref, z_ref = refs[nb:]
    back = back_ref[...]
    rows, lanes = q_ref.shape
    span = filt_ref.shape[1]

    def conv(i, sl):
        ext = jnp.concatenate(
            [edge_ref[i, :, sl].astype(jnp.float32)]
            + [b[0, i, :, sl].astype(jnp.float32) for b in block_refs],
            axis=0,
        )
        total = filt_ref[i, 0:1, sl] * ext[EDGE:]
        for j in range(1, span):
            piece = ext[EDGE - j : EDGE - j + rows]
            total = total + filt_ref[i, j : j + 1, sl] * jnp.where(back >= j, piece, 0.0)
        return total

    for lo in range(0, lanes, 128):
        sl = slice(lo, lo + 128)
        q_ref[:, sl] = conv(0, sl)
        z_ref[:, sl] = (conv(1, sl) * conv(2, sl)).astype(z_ref.dtype)


def short_stage(incoming, wanted, edge, filt, back):
    n, _, blk, width = incoming.shape
    nb = wanted.shape[0]
    rows = nb * blk
    lanes = 256
    in_specs = [
        pl.BlockSpec((1, 3, blk, lanes), functools.partial(lambda k, i, w: (w[k], 0, 0, i), k))
        for k in range(nb)
    ] + [
        pl.BlockSpec((3, EDGE, lanes), lambda i, w: (0, 0, i)),
        pl.BlockSpec((3, filt.shape[1], lanes), lambda i, w: (0, 0, i)),
        pl.BlockSpec((rows, 128), lambda i, w: (0, 0)),
    ]
    return pl.pallas_call(
        functools.partial(short_kernel, nb),
        grid_spec=pltpu.PrefetchScalarGridSpec(
            num_scalar_prefetch=1,
            grid=(width // lanes,),
            in_specs=in_specs,
            out_specs=[
                pl.BlockSpec((rows, lanes), lambda i, w: (0, i)),
                pl.BlockSpec((rows, lanes), lambda i, w: (0, i)),
            ],
        ),
        out_shape=[
            jax.ShapeDtypeStruct((rows, width), jnp.float32),
            jax.ShapeDtypeStruct((rows, width), jnp.bfloat16),
        ],
        compiler_params=pltpu.CompilerParams(vmem_limit_bytes=48 * 2**20),
        name="short_conv",
    )(wanted, *([incoming] * nb), edge, filt, back)


def medium_kernel(per_group, span, prev_ref, z_ref, q_ref, skip_ref, line_ref, back_ref, h_ref):
    rows, lanes = z_ref.shape
    row = lax.broadcasted_iota(jnp.int32, (span, 2 * span), 0)
    col = lax.broadcasted_iota(jnp.int32, (span, 2 * span), 1)
    step = span + row - col
    lane = lax.broadcasted_iota(jnp.int32, (span, 128), 1)
    tiles = rows // span
    keeps = [
        step <= jnp.concatenate([back_ref[r * span : (r + 1) * span]] * 2, axis=1)
        for r in range(tiles)
    ]
    groups = 128 // per_group
    for lo in range(0, lanes, 128):
        sl = slice(lo, lo + 128)
        ext = jnp.concatenate([prev_ref[:, sl], z_ref[:, sl]], axis=0)
        total = [jnp.zeros((span, 128), jnp.float32) for _ in range(tiles)]
        for g in range(groups):
            line = line_ref[0, lo // per_group + g : lo // per_group + g + 1, :]
            band = pltpu.roll(
                jnp.broadcast_to(line, (span, 2 * span)), 0, 1, stride=1, stride_axis=0
            )
            mine = (lane >= g * per_group) & (lane < (g + 1) * per_group)
            for r in range(tiles):
                kept = jnp.where(keeps[r], band, 0.0).astype(jnp.bfloat16)
                part = jnp.dot(
                    kept,
                    ext[r * span : (r + 2) * span],
                    preferred_element_type=jnp.float32,
                )
                total[r] = jnp.where(mine, part, total[r])
        for r in range(tiles):
            rs = slice(r * span, (r + 1) * span)
            full = total[r] + skip_ref[0:1, sl] * z_ref[rs, sl].astype(jnp.float32)
            h_ref[rs, sl] = (q_ref[rs, sl] * full).astype(h_ref.dtype)


def medium_stage(z_prev, z_vals, query, skip, taps, back):
    rows, width = z_vals.shape
    span, groups = taps.shape
    per_group = width // groups
    lanes = 256
    line = jnp.concatenate(
        [
            jnp.zeros((groups, 1), jnp.float32),
            jnp.transpose(taps[::-1]).astype(jnp.float32),
            jnp.zeros((groups, span - 1), jnp.float32),
        ],
        axis=1,
    ).reshape(width // lanes, lanes // per_group, 2 * span)
    return pl.pallas_call(
        functools.partial(medium_kernel, per_group, span),
        grid=(width // lanes,),
        in_specs=[
            pl.BlockSpec((span, lanes), lambda i: (0, i)),
            pl.BlockSpec((rows, lanes), lambda i: (0, i)),
            pl.BlockSpec((rows, lanes), lambda i: (0, i)),
            pl.BlockSpec((1, lanes), lambda i: (0, i)),
            pl.BlockSpec((1, lanes // per_group, 2 * span), lambda i: (i, 0, 0)),
            pl.BlockSpec((rows, 128), lambda i: (0, 0)),
        ],
        out_specs=pl.BlockSpec((rows, lanes), lambda i: (0, i)),
        out_shape=jax.ShapeDtypeStruct((rows, width), jnp.bfloat16),
        compiler_params=pltpu.CompilerParams(vmem_limit_bytes=48 * 2**20),
        name="medium_conv",
    )(z_prev, z_vals, query, skip, line, back)


def project_kernel(
    n, m, hid_ref, w_ref, out_ref, hid, pout, pin, zin,
    own_sem, hsend, hrecv, psend, precv, zsend, zrecv,
):
    c = lax.axis_index("ctx")
    z = lax.axis_index("mp")
    share = n // m
    rows = hid_ref.shape[0]
    cols = w_ref.shape[1]

    barrier = pltpu.get_barrier_semaphore()
    for d in range(1, n):
        pl.semaphore_signal(barrier, inc=1, device_id=(flipped(c, d), z), device_id_type=MESH)
    for s in range(1, m):
        pl.semaphore_signal(barrier, inc=1, device_id=(c, flipped(z, s)), device_id_type=MESH)
    pl.semaphore_wait(barrier, n - 1 + m - 1)

    sent = []

    def send_hidden(origin, peer, slot, src):
        copy = pltpu.make_async_remote_copy(
            src_ref=src,
            dst_ref=hid.at[origin],
            send_sem=hsend.at[slot],
            recv_sem=hrecv.at[origin],
            device_id=(peer, z),
            device_id_type=MESH,
        )
        copy.start()
        sent.append(copy)

    def hidden_arrived(origin):
        pltpu.make_async_remote_copy(
            src_ref=hid_ref,
            dst_ref=hid.at[origin],
            send_sem=hsend.at[0],
            recv_sem=hrecv.at[origin],
            device_id=(flipped(c, 1), z),
            device_id_type=MESH,
        ).wait_recv()

    def multiply(origin, d, src):
        @pl.loop(0, cols // 256)
        def _(i):
            at = pl.ds(pl.multiple_of(i * 256, 256), 256)
            pout[d, :, at] = jnp.dot(
                src[...], w_ref[:, at], preferred_element_type=jnp.float32
            ).astype(jnp.bfloat16)

        if d == 0:
            copy = pltpu.make_async_copy(pout.at[0], pin.at[c], precv.at[c])
        else:
            copy = pltpu.make_async_remote_copy(
                src_ref=pout.at[d],
                dst_ref=pin.at[c],
                send_sem=psend.at[d],
                recv_sem=precv.at[c],
                device_id=(origin, z),
                device_id_type=MESH,
            )
            sent.append(copy)
        copy.start()

    mate = flipped(c, 1)
    if n == 8:
        core = c % 2
        x_peer, y_peer = flipped(c, 2), flipped(c, 4)
        first = x_peer + (y_peer - x_peer) * core
        second = y_peer + (x_peer - y_peer) * core
        across = flipped(c, 6)
        send_hidden(c, first, 1, hid_ref)
        send_hidden(c, second, 2, hid_ref)
        send_hidden(c, mate, 3, hid_ref)
        multiply(c, 0, hid_ref)
        hidden_arrived(first)
        send_hidden(first, second, 4, hid.at[first])
        send_hidden(first, mate, 5, hid.at[first])
        hidden_arrived(second)
        send_hidden(second, mate, 6, hid.at[second])
        hidden_arrived(mate)
        multiply(mate, 1, hid.at[mate])
        multiply(first, 2, hid.at[first])
        multiply(second, 4, hid.at[second])
        hidden_arrived(flipped(second, 1))
        multiply(flipped(second, 1), 5, hid.at[flipped(second, 1)])
        hidden_arrived(flipped(first, 1))
        multiply(flipped(first, 1), 3, hid.at[flipped(first, 1)])
        hidden_arrived(across)
        send_hidden(across, mate, 7, hid.at[across])
        multiply(across, 6, hid.at[across])
        hidden_arrived(flipped(across, 1))
        multiply(flipped(across, 1), 7, hid.at[flipped(across, 1)])
    else:
        for d in range(1, n):
            send_hidden(c, flipped(c, d), d, hid_ref)
        multiply(c, 0, hid_ref)
        for d in range(1, n):
            origin = flipped(c, d)
            hidden_arrived(origin)
            multiply(origin, d, hid.at[origin])

    home = lax.div(c, share)

    def forward(plane, t, h):
        return pltpu.make_async_remote_copy(
            src_ref=pin.at[plane * share + h],
            dst_ref=zin.at[z, h],
            send_sem=zsend.at[t, h],
            recv_sem=zrecv.at[z, h],
            device_id=(c, plane),
            device_id_type=MESH,
        )

    for t in range(m):
        plane = flipped(home, t)
        for h in range(share):
            block = plane * share + h
            pltpu.make_async_copy(pout.at[0], pin.at[block], precv.at[block]).wait()

            @pl.when(plane != z)
            def _(plane=plane, t=t, h=h):
                forward(plane, t, h).start()

    for s in range(1, m):
        other = flipped(z, s)
        for h in range(share):
            pltpu.make_async_remote_copy(
                src_ref=pin.at[0],
                dst_ref=zin.at[other, h],
                send_sem=zsend.at[0, 0],
                recv_sem=zrecv.at[other, h],
                device_id=(c, other),
                device_id_type=MESH,
            ).wait_recv()
    for h in range(share):
        total = pin[z * share + h].astype(jnp.float32)
        for s in range(1, m):
            total = total + zin[flipped(z, s), h].astype(jnp.float32)
        out_ref[:, h * cols : (h + 1) * cols] = total.astype(out_ref.dtype)

    for copy in sent:
        copy.wait_send()
    for t in range(m):
        plane = flipped(home, t)
        for h in range(share):

            @pl.when(plane != z)
            def _(plane=plane, t=t, h=h):
                forward(plane, t, h).wait_send()


def project(hidden, weight):
    n, m = lax.axis_size("ctx"), lax.axis_size("mp")
    share = n // m
    rows, depth = hidden.shape
    cols = weight.shape[1]
    bf16 = jnp.bfloat16
    dma = pltpu.SemaphoreType.DMA
    return pl.pallas_call(
        functools.partial(project_kernel, n, m),
        out_shape=jax.ShapeDtypeStruct((rows, share * cols), bf16),
        in_specs=[pl.BlockSpec(memory_space=pltpu.VMEM)] * 2,
        out_specs=pl.BlockSpec(memory_space=pltpu.VMEM),
        scratch_shapes=[
            pltpu.VMEM((n, rows, depth), bf16),
            pltpu.VMEM((n, rows, cols), bf16),
            pltpu.VMEM((n, rows, cols), bf16),
            pltpu.VMEM((m, share, rows, cols), bf16),
            dma,
            dma((n,)),
            dma((n,)),
            dma((n,)),
            dma((n,)),
            dma((m, share)),
            dma((m, share)),
        ],
        compiler_params=pltpu.CompilerParams(
            collective_id=1, has_side_effects=True, vmem_limit_bytes=50 * 2**20
        ),
        name="project",
    )(hidden, weight)


def on_device(
    source_rows,
    short_filters,
    medium_filters,
    skip_gain,
    out_weight,
    doc_lengths,
    block_packing_device,
):
    stretches = lax.axis_size("ctx")
    me = lax.axis_index("ctx")
    nb_own = block_packing_device.shape[1]
    blk = source_rows.shape[0] // stretches
    rows = nb_own * blk
    width = source_rows.shape[2]
    mr_len = medium_filters.shape[0]
    member = jnp.any(block_packing_device == me, axis=1)
    flags = member.astype(jnp.int32)
    slots = jnp.minimum(jnp.cumsum(flags) - flags, stretches - 1)
    blocks = source_rows.reshape(stretches, blk, 3, width)
    outgoing = jnp.take(blocks, slots, axis=0, mode="clip").transpose(0, 2, 1, 3)
    incoming = exchange(outgoing)
    wanted = lax.dynamic_index_in_dim(block_packing_device, me, 0, keepdims=False)

    ends = jnp.cumsum(doc_lengths)
    starts = ends - doc_lengths
    positions = me * rows + jnp.arange(rows, dtype=jnp.int32)
    begin = jnp.max(jnp.where(starts[None, :] <= positions[:, None], starts[None, :], 0), axis=1)
    back = jnp.broadcast_to((positions - begin)[:, None], (rows, 128))

    last = lax.dynamic_index_in_dim(incoming, wanted[nb_own - 1], 0, keepdims=False)
    edge = passed_along(last[:, blk - EDGE :], "ctx", 1)
    query, z_vals = short_stage(incoming, wanted, edge, short_filters.astype(jnp.float32), back)
    z_prev = passed_along(z_vals[rows - mr_len :], "ctx", 1)
    hidden = medium_stage(z_prev, z_vals, query, skip_gain[None, :], medium_filters, back)
    return project(hidden, out_weight)


def solution(mesh):
    return jax.shard_map(
        on_device,
        mesh=mesh,
        in_specs=(
            P("ctx", None, "mp"),
            P(None, None, "mp"),
            P(None, "mp"),
            P("mp"),
            P("mp", "ctx"),
            P(),
            P(),
        ),
        out_specs=P("ctx", "mp"),
        check_vma=False,
    )
```

time: 375 us -> 288 us (0.77)
  Pallas kernels: 0 us -> 257 us
  waiting for transfers between devices: 190 us -> 8.31 us
  local copies, waits for them, and re-layouts: 98.3 us -> 11.1 us
  matrix products: 38.1 us -> 0 us
  other arithmetic: 16.8 us -> 1.35 us
  between operations: 13.6 us -> 2.1 us
  starting transfers between devices: 14.7 us -> 6.95 us
    pallas_call x0 -> x4, Pallas kernels: none -> 257 us  [the longest x1 167 us: project(): pl.pallas_call(functools.partial(project_kernel, n, m), out_shape=jax.Sha...]
    all_to_all x1 -> x0, waiting for transfers between devices: 108 us -> none  [on_device(): lax.all_to_all(outgoing, 'ctx', split_axis=0, concat_axis=0, tiled=True)]
    reduce_scatter x1 -> x0, waiting for transfers between devices: 78.5 us -> none  [on_device(): lax.psum_scatter(partial_value.astype(jnp.bfloat16), 'mp', scatter_dimens...]
    reshape x3 -> x0, local copies, waits for them, and re-layouts: 67.3 us -> none  [the longest x2 64.4 us: on_device(): jnp.tile(line, (1, rows + 1))[:, :rows * span_cols]]
    dot_general x2 -> x0, matrix products: 38.1 us -> none  [the longest x1 25 us: on_device(): jnp.dot(hidden, lax.all_gather(out_weight, 'ctx', axis=1, tiled=True), pr...]
    slice x5 -> x3, local copies, waits for them, and re-layouts: 10.6 us -> 1.36 us  [the longest x1 0.83 us: on_device(): z_prev = passed_along(z_vals[rows - mr_len:], 'ctx', 1)]
    select_n x4 -> x0, other arithmetic: 7.8 us -> none  [the longest x1 7.28 us: on_device(): jnp.where(member[:, None, None, None], jnp.take(blocks, slots, axis=0), j...]
    another operation x1 -> x0, local copies, waits for them, and re-layouts: 6.44 us -> none  [on_device(): jnp.tile(line, (1, rows + 1))[:, :rows * span_cols]]
  transfers between devices with their start and end apart: 5 -> 2, of which waited for: 3 -> 2; matrix products, arithmetic and copies ran while one was open for 34% -> 0% of each run, Pallas kernels for 0% -> 0%
where the time goes in v1:
time: 288 us; the launch traced here: 287 us
  Pallas kernels  257 us (89%)
  local copies, waits for them, and re-layouts  11.1 us (4%)
  waiting for transfers between devices  8.31 us (3%)
  starting transfers between devices  6.95 us (2%)
    pallas_call x1, Pallas kernels, project(): pl.pallas_call(functools.partial(project_kernel, n, m), out_shape=jax.Sha...  167 us
    pallas_call x1, Pallas kernels, exchange(): pl.pallas_call(functools.partial(exchange_kernel, n), out_shape=jax.Shape...  72.1 us
    pallas_call x1, Pallas kernels, short_stage(): pl.pallas_call(functools.partial(short_kernel, nb), grid_spec=pltpu.Prefe...  10.4 us
    ppermute x2, waiting for transfers between devices, passed_along(): return lax.ppermute(block, axis, route)  8.31 us
    pallas_call x1, Pallas kernels, medium_stage(): pl.pallas_call(functools.partial(medium_kernel, per_group, span), grid=(w...  7.69 us
    ppermute x2, starting transfers between devices, passed_along(): return lax.ppermute(block, axis, route)  6.95 us
    gather x1, local copies, waits for them, and re-layouts, on_device(): jnp.take(blocks, slots, axis=0, mode='clip').transpose(0, 2, 1, 3)  6.39 us
  transfers between devices with their start and end apart: 2, of which 2 were waited for; matrix products, arithmetic and copies ran while one was open for 0% of the time, Pallas kernels for 0%

profile of v1, /device:TPU:13, one launch (start us, length us, event | category | flops | bytes accessed | tf_op | source)
XLA Modules:
  0.0 287.1 jit_solution(16761998328483408438)
XLA Ops:
  0.0 0.9 fusion.1
  0.9 0.5 slice.10
  2.7 0.7 compare_reduce_fusion
  3.4 0.2 reduce-window.14
  3.6 6.4 %gather_fusion = bf16[8,64,3,2048]{3,1,2,0:T(8,128)(2,1)} fusion(bf16[8,64,3,2048]{3,1,0,2:T(8,128)(2,1)} %bitcast.22, s32[1024]{0:T(1024)S(1)} %pad_clamp_fusion), kind=kCustom, calls=%fused_computation | custom fusion | bytes 12582944 | tf_op jit(solution)/shard_map/jit(_take)/gather | solution.py:409
  10.0 0.0 copy-start.3
  10.0 0.0 copy-start.1
  10.0 72.1 %exchange.1.refs_0_.refs_1_.refs_2_.refs_3_ = bf16[8,3,64,2048]{3,2,1,0:T(8,128)(2,1)} custom-call(bf16[8,3,64,2048]{3,2,1,0:T(8,128)(2,1)} %bitcast.21), custom_call_target="tpu_custom_call" | custom-call | tf_op jit(solution)/shard_map/exchange/pallas_call | solution.py:66
  82.7 1.2 dynamic-slice_bitcast_fusion
  83.9 2.6 collective-permute-start
  86.5 0.0 copy-done.3
  86.5 0.2 reduce-window.15
  86.7 0.0 copy-done.1
  86.8 0.1 select_reduce_fusion
  86.9 2.3 collective-permute-done.refs_4_
  89.1 0.1 broadcast_in_dim.31.refs_6_.back_ref
  89.2 0.0 copy-start.2
  89.2 0.0 copy-start
  89.2 10.4 %short_conv.1 = (f32[256,2048]{1,0:T(8,128)S(1)}, bf16[256,2048]{1,0:T(8,128)(2,1)S(1)}) custom-call(s32[4]{0:T(128)S(1)} %get-tuple-element.9.wanted_ref, bf16[8,3,64,2048]{3,2,1,0:T(8,128)(2,1)} %exchange.1.refs_0_.refs_1_.refs_2_.refs_3_, bf16[8,3,64,2048]{3,2,1,0:T(8,128)(2,1)} %exchange.1.refs_0_.refs_1_.refs_2_.refs_3_, ...), custom_call_target="tpu_custom_call" | custom-call | tf_op jit(solution)/shard_map/short_conv/pallas_call | solution.py:119
  99.7 0.8 slice.12
  100.5 4.4 %collective-permute-start.1 = (bf16[128,2048]{1,0:T(8,128)(2,1)}, bf16[128,2048]{1,0:T(8,128)(2,1)}, u32[]{:S(2)}, u32[]{:S(2)}) collective-permute-start(bf16[128,2048]{1,0:T(8,128)(2,1)} %slice.12), channel_id=1, source_target_pairs={{0,4},{4,8},{8,12},{12,16},{16,20},{20,24},{24,28},{1,5},{5,9},{9,... | collective-permute-start | bytes 1572872 | tf_op jit(solution)/shard_map/ppermute | solution.py:26
  104.9 0.0 copy-done.2
  104.9 0.1 pad.2.clone
  105.0 0.1 maximum_maximum_fusion
  105.1 0.1 copy.9
  105.3 6.0 %collective-permute-done.1.prev_ref = bf16[128,2048]{1,0:T(8,128)(2,1)} collective-permute-done((bf16[128,2048]{1,0:T(8,128)(2,1)}, bf16[128,2048]{1,0:T(8,128)(2,1)}, u32[]{:S(2)}, u32[]{:S(2)}) %collective-permute-start.1) | collective-permute-done | bytes 524320 | tf_op jit(solution)/shard_map/ppermute | solution.py:26
  111.3 0.0 copy-done
  111.3 7.7 %medium_conv.1.hid_ref = bf16[256,2048]{1,0:T(8,128)(2,1)S(1)} custom-call(bf16[128,2048]{1,0:T(8,128)(2,1)} %collective-permute-done.1.prev_ref, bf16[256,2048]{1,0:T(8,128)(2,1)S(1)} %get-tuple-element.7.z_ref, f32[256,2048]{1,0:T(8,128)S(1)} %get-tuple-element.8.q_ref, f32[1,2048]{1,0:T(1,128)S(1)} %bitcast.20, f32[8,16,256]{2,1,0:T(8,128)S(1)} %bitcast.19, ...), custom_call_target="tpu_custom_call" | custom-call | tf_op jit(solution)/shard_map/medium_conv/pallas_call | solution.py:188
  119.0 167.1 %project.1 = bf16[256,2048]{1,0:T(8,128)(2,1)S(1)} custom-call(bf16[256,2048]{1,0:T(8,128)(2,1)S(1)} %medium_conv.1.hid_ref, bf16[2048,1024]{1,0:T(8,128)(2,1)} %w_ref.1), custom_call_target="tpu_custom_call" | custom-call | tf_op jit(solution)/shard_map/project/pallas_call | solution.py:364
  286.1 1.0 copy.11
  (12 shorter events, 0.1 us)
Async XLA Ops:
  10.0 76.6 %copy-start.3 = (s32[8]{0:T(128)S(1)}, s32[8]{0:T(128)}, u32[]{:S(2)}) copy-start(s32[8]{0:T(128)} %param.12) | copy-start | bytes 100
  10.0 76.8 %copy-start.1 = (bf16[3,7,2048]{2,1,0:T(8,128)(2,1)S(1)}, bf16[3,7,2048]{2,1,0:T(8,128)(2,1)}, u32[]{:S(2)}) copy-start(bf16[3,7,2048]{2,1,0:T(8,128)(2,1)} %param.8) | copy-start | bytes 258052
  83.9 5.2 %collective-permute-start = (bf16[3,16,2048]{2,1,0:T(8,128)(2,1)S(1)}, bf16[3,16,2048]{2,1,0:T(8,128)(2,1)S(1)}, u32[]{:S(2)}, u32[]{:S(2)}) collective-permute-start(bf16[3,16,2048]{2,1,0:T(8,128)(2,1)S(1)} %slice.15), channel_id=1, source_target_pairs={{0,4},{4,8},{8,12},{12,16},{16,20},{20,24},{24,28},{1,5},{5,9},{9,... | collective-permute-start | bytes 589832 | tf_op jit(solution)/shard_map/ppermute | solution.py:26
  89.2 15.7 %copy-start.2 = (bf16[128,128]{1,0:T(8,128)(2,1)S(1)}, bf16[128,128]{1,0:T(8,128)(2,1)}, u32[]{:S(2)}) copy-start(bf16[128,128]{1,0:T(8,128)(2,1)} %param.9) | copy-start | bytes 98308
  89.2 22.1 %copy-start = (f32[2048]{0:T(1024)S(1)}, f32[2048]{0:T(1024)}, u32[]{:S(2)}) copy-start(f32[2048]{0:T(1024)} %param.10) | copy-start | bytes 24580
  100.5 10.8 %collective-permute-start.1 = (bf16[128,2048]{1,0:T(8,128)(2,1)}, bf16[128,2048]{1,0:T(8,128)(2,1)}, u32[]{:S(2)}, u32[]{:S(2)}) collective-permute-start(bf16[128,2048]{1,0:T(8,128)(2,1)} %slice.12), channel_id=1, source_target_pairs={{0,4},{4,8},{8,12},{12,16},{16,20},{20,24},{24,28},{1,5},{5,9},{9,... | collective-permute-start | bytes 1572872 | tf_op jit(solution)/shard_map/ppermute | solution.py:26

commit v2 on v1

--- a/solution.py
+++ b/solution.py
@@ -204,14 +204,19 @@
 
 
 def project_kernel(
-    n, m, hid_ref, w_ref, out_ref, hid, pout, pin, zin,
-    own_sem, hsend, hrecv, psend, precv, zsend, zrecv,
+    n, m, hid_ref, w_ref, out_ref, hid, pout, near_in, far_out, far_in, keep, fin, xin,
+    hsend, hrecv, nsend, nrecv, fsend, frecv, xsend, xrecv, osend, orecv,
 ):
     c = lax.axis_index("ctx")
     z = lax.axis_index("mp")
     share = n // m
     rows = hid_ref.shape[0]
     cols = w_ref.shape[1]
+    part = rows // m
+    halving = m == 4
+
+    def part_rows(index):
+        return pl.ds(pl.multiple_of(index * part, part), part)
 
     barrier = pltpu.get_barrier_semaphore()
     for d in range(1, n):
@@ -222,49 +227,52 @@
 
     sent = []
 
-    def send_hidden(origin, peer, slot, src):
-        copy = pltpu.make_async_remote_copy(
+    def remote(src, dst, send_sem, recv_sem, device):
+        return pltpu.make_async_remote_copy(
             src_ref=src,
-            dst_ref=hid.at[origin],
-            send_sem=hsend.at[slot],
-            recv_sem=hrecv.at[origin],
-            device_id=(peer, z),
+            dst_ref=dst,
+            send_sem=send_sem,
+            recv_sem=recv_sem,
+            device_id=device,
             device_id_type=MESH,
         )
+
+    def send(*args):
+        copy = remote(*args)
         copy.start()
         sent.append(copy)
 
+    def send_hidden(origin, peer, slot, src):
+        send(src, hid.at[origin], hsend.at[slot], hrecv.at[origin], (peer, z))
+
     def hidden_arrived(origin):
-        pltpu.make_async_remote_copy(
-            src_ref=hid_ref,
-            dst_ref=hid.at[origin],
-            send_sem=hsend.at[0],
-            recv_sem=hrecv.at[origin],
-            device_id=(flipped(c, 1), z),
-            device_id_type=MESH,
+        remote(
+            hid_ref, hid.at[origin], hsend.at[0], hrecv.at[origin], (flipped(c, 1), z)
         ).wait_recv()
 
-    def multiply(origin, d, src):
+    origins = []
+
+    def multiply(origin, src):
+        i = len(origins)
+        origins.append(origin)
+
         @pl.loop(0, cols // 256)
-        def _(i):
-            at = pl.ds(pl.multiple_of(i * 256, 256), 256)
-            pout[d, :, at] = jnp.dot(
+        def _(k):
+            at = pl.ds(pl.multiple_of(k * 256, 256), 256)
+            pout[i, :, at] = jnp.dot(
                 src[...], w_ref[:, at], preferred_element_type=jnp.float32
             ).astype(jnp.bfloat16)
 
-        if d == 0:
-            copy = pltpu.make_async_copy(pout.at[0], pin.at[c], precv.at[c])
-        else:
-            copy = pltpu.make_async_remote_copy(
-                src_ref=pout.at[d],
-                dst_ref=pin.at[c],
-                send_sem=psend.at[d],
-                recv_sem=precv.at[c],
-                device_id=(origin, z),
-                device_id_type=MESH,
+        for s in [3, 1] if halving else range(1, m):
+            slot = s // 2 if halving else s - 1
+            peer = flipped(z, 1) if halving else flipped(z, s)
+            send(
+                pout.at[i, part_rows(flipped(z, s))],
+                near_in.at[i, slot],
+                nsend.at[i, slot],
+                nrecv.at[i, slot],
+                (c, peer),
             )
-            sent.append(copy)
-        copy.start()
 
     mate = flipped(c, 1)
     if n == 8:
@@ -276,72 +284,103 @@
         send_hidden(c, first, 1, hid_ref)
         send_hidden(c, second, 2, hid_ref)
         send_hidden(c, mate, 3, hid_ref)
-        multiply(c, 0, hid_ref)
+        multiply(c, hid_ref)
+        hidden_arrived(mate)
+        multiply(mate, hid.at[mate])
         hidden_arrived(first)
         send_hidden(first, second, 4, hid.at[first])
         send_hidden(first, mate, 5, hid.at[first])
         hidden_arrived(second)
         send_hidden(second, mate, 6, hid.at[second])
-        hidden_arrived(mate)
-        multiply(mate, 1, hid.at[mate])
-        multiply(first, 2, hid.at[first])
-        multiply(second, 4, hid.at[second])
-        hidden_arrived(flipped(second, 1))
-        multiply(flipped(second, 1), 5, hid.at[flipped(second, 1)])
-        hidden_arrived(flipped(first, 1))
-        multiply(flipped(first, 1), 3, hid.at[flipped(first, 1)])
+        multiply(first, hid.at[first])
+        multiply(second, hid.at[second])
+        for origin in (flipped(second, 1), flipped(first, 1)):
+            hidden_arrived(origin)
+            multiply(origin, hid.at[origin])
         hidden_arrived(across)
         send_hidden(across, mate, 7, hid.at[across])
-        multiply(across, 6, hid.at[across])
+        multiply(across, hid.at[across])
         hidden_arrived(flipped(across, 1))
-        multiply(flipped(across, 1), 7, hid.at[flipped(across, 1)])
+        multiply(flipped(across, 1), hid.at[flipped(across, 1)])
     else:
         for d in range(1, n):
             send_hidden(c, flipped(c, d), d, hid_ref)
-        multiply(c, 0, hid_ref)
+        multiply(c, hid_ref)
         for d in range(1, n):
             origin = flipped(c, d)
             hidden_arrived(origin)
-            multiply(origin, d, hid.at[origin])
+            multiply(origin, hid.at[origin])
+
+    def near_arrived(i, slot):
+        remote(
+            pout.at[i, part_rows(0)],
+            near_in.at[i, slot],
+            nsend.at[i, slot],
+            nrecv.at[i, slot],
+            (c, flipped(z, 1)),
+        ).wait_recv()
+
+    def finish(i, total):
+        fin[i] = total.astype(jnp.bfloat16)
+        if i == 0:
+            pltpu.make_async_copy(fin.at[0], xin.at[c], xrecv.at[c]).start()
+        else:
+            send(fin.at[i], xin.at[c], xsend.at[i], xrecv.at[c], (origins[i], z))
+
+    if halving:
+        far = flipped(z, 2)
+        for i in range(n):
+            near_arrived(i, 1)
+            far_out[i] = (
+                pout[i, part_rows(far)].astype(jnp.float32) + near_in[i, 1].astype(jnp.float32)
+            ).astype(jnp.bfloat16)
+            send(far_out.at[i], far_in.at[i], fsend.at[i], frecv.at[i], (c, far))
+            near_arrived(i, 0)
+            keep[i] = pout[i, part_rows(z)].astype(jnp.float32) + near_in[i, 0].astype(jnp.float32)
+        for i in range(n):
+            remote(far_out.at[i], far_in.at[i], fsend.at[i], frecv.at[i], (c, far)).wait_recv()
+            finish(i, keep[i] + far_in[i].astype(jnp.float32))
+    else:
+        for i in range(n):
+            total = pout[i, part_rows(z)].astype(jnp.float32)
+            for s in range(1, m):
+                near_arrived(i, s - 1)
+                total = total + near_in[i, s - 1].astype(jnp.float32)
+            finish(i, total)
 
     home = lax.div(c, share)
 
     def forward(plane, t, h):
-        return pltpu.make_async_remote_copy(
-            src_ref=pin.at[plane * share + h],
-            dst_ref=zin.at[z, h],
-            send_sem=zsend.at[t, h],
-            recv_sem=zrecv.at[z, h],
-            device_id=(c, plane),
-            device_id_type=MESH,
+        return remote(
+            xin.at[plane * share + h],
+            out_ref.at[part_rows(z), pl.ds(h * cols, cols)],
+            osend.at[t, h],
+            orecv.at[z, h],
+            (c, plane),
         )
 
     for t in range(m):
         plane = flipped(home, t)
         for h in range(share):
             block = plane * share + h
-            pltpu.make_async_copy(pout.at[0], pin.at[block], precv.at[block]).wait()
+            pltpu.make_async_copy(fin.at[0], xin.at[block], xrecv.at[block]).wait()
 
             @pl.when(plane != z)
             def _(plane=plane, t=t, h=h):
                 forward(plane, t, h).start()
 
+    for h in range(share):
+        out_ref[part_rows(z), pl.ds(h * cols, cols)] = xin[z * share + h]
     for s in range(1, m):
         other = flipped(z, s)
         for h in range(share):
-            pltpu.make_async_remote_copy(
-                src_ref=pin.at[0],
-                dst_ref=zin.at[other, h],
-                send_sem=zsend.at[0, 0],
-                recv_sem=zrecv.at[other, h],
-                device_id=(c, other),
-                device_id_type=MESH,
+            remote(
+                xin.at[0],
+                out_ref.at[part_rows(other), pl.ds(h * cols, cols)],
+                osend.at[0, 0],
+                orecv.at[other, h],
+                (c, other),
             ).wait_recv()
-    for h in range(share):
-        total = pin[z * share + h].astype(jnp.float32)
-        for s in range(1, m):
-            total = total + zin[flipped(z, s), h].astype(jnp.float32)
-        out_ref[:, h * cols : (h + 1) * cols] = total.astype(out_ref.dtype)
 
     for copy in sent:
         copy.wait_send()
@@ -359,6 +398,8 @@
     share = n // m
     rows, depth = hidden.shape
     cols = weight.shape[1]
+    part = rows // m
+    near = 2 if m == 4 else m - 1
     bf16 = jnp.bfloat16
     dma = pltpu.SemaphoreType.DMA
     return pl.pallas_call(
@@ -369,9 +410,16 @@
         scratch_shapes=[
             pltpu.VMEM((n, rows, depth), bf16),
             pltpu.VMEM((n, rows, cols), bf16),
-            pltpu.VMEM((n, rows, cols), bf16),
-            pltpu.VMEM((m, share, rows, cols), bf16),
-            dma,
+            pltpu.VMEM((n, near, part, cols), bf16),
+            pltpu.VMEM((n, part, cols), bf16),
+            pltpu.VMEM((n, part, cols), bf16),
+            pltpu.VMEM((n, part, cols), jnp.float32),
+            pltpu.VMEM((n, part, cols), bf16),
+            pltpu.VMEM((n, part, cols), bf16),
+            dma((n,)),
+            dma((n,)),
+            dma((n, near)),
+            dma((n, near)),
             dma((n,)),
             dma((n,)),
             dma((n,)),

time: 288 us -> 242 us (0.84)
  Pallas kernels: 257 us -> 211 us
    pallas_call x1, Pallas kernels: 167 us -> 121 us  [project(): pl.pallas_call(functools.partial(project_kernel, n, m), out_shape=jax.Sha...]
where the time goes in v2:
time: 242 us; the launch traced here: 241 us
  Pallas kernels  211 us (87%)
  local copies, waits for them, and re-layouts  11.1 us (5%)
  waiting for transfers between devices  8.31 us (3%)
  starting transfers between devices  6.95 us (3%)
    pallas_call x1, Pallas kernels, project(): pl.pallas_call(functools.partial(project_kernel, n, m), out_shape=jax.Sha...  121 us
    pallas_call x1, Pallas kernels, exchange(): pl.pallas_call(functools.partial(exchange_kernel, n), out_shape=jax.Shape...  72.1 us
    pallas_call x1, Pallas kernels, short_stage(): pl.pallas_call(functools.partial(short_kernel, nb), grid_spec=pltpu.Prefe...  10.4 us
    ppermute x2, waiting for transfers between devices, passed_along(): return lax.ppermute(block, axis, route)  8.31 us
    pallas_call x1, Pallas kernels, medium_stage(): pl.pallas_call(functools.partial(medium_kernel, per_group, span), grid=(w...  7.69 us
    ppermute x2, starting transfers between devices, passed_along(): return lax.ppermute(block, axis, route)  6.95 us
    gather x1, local copies, waits for them, and re-layouts, on_device(): jnp.take(blocks, slots, axis=0, mode='clip').transpose(0, 2, 1, 3)  6.39 us
  transfers between devices with their start and end apart: 2, of which 2 were waited for; matrix products, arithmetic and copies ran while one was open for 0% of the time, Pallas kernels for 0%

profile of v2, /device:TPU:13, one launch (start us, length us, event | category | flops | bytes accessed | tf_op | source)
XLA Modules:
  0.0 240.8 jit_solution(7240076826522820213)
XLA Ops:
  0.0 0.9 fusion.1
  0.9 0.5 slice.10
  2.7 0.7 compare_reduce_fusion
  3.4 0.2 reduce-window.14
  3.6 6.4 %gather_fusion = bf16[8,64,3,2048]{3,1,2,0:T(8,128)(2,1)} fusion(bf16[8,64,3,2048]{3,1,0,2:T(8,128)(2,1)} %bitcast.22, s32[1024]{0:T(1024)S(1)} %pad_clamp_fusion), kind=kCustom, calls=%fused_computation | custom fusion | bytes 12582944 | tf_op jit(solution)/shard_map/jit(_take)/gather | solution.py:457
  10.0 0.0 copy-start.3
  10.0 0.0 copy-start.1
  10.0 72.1 %exchange.1.refs_0_.refs_1_.refs_2_.refs_3_ = bf16[8,3,64,2048]{3,2,1,0:T(8,128)(2,1)} custom-call(bf16[8,3,64,2048]{3,2,1,0:T(8,128)(2,1)} %bitcast.21), custom_call_target="tpu_custom_call" | custom-call | tf_op jit(solution)/shard_map/exchange/pallas_call | solution.py:66
  82.7 1.2 dynamic-slice_bitcast_fusion
  83.9 2.6 %collective-permute-start = (bf16[3,16,2048]{2,1,0:T(8,128)(2,1)S(1)}, bf16[3,16,2048]{2,1,0:T(8,128)(2,1)S(1)}, u32[]{:S(2)}, u32[]{:S(2)}) collective-permute-start(bf16[3,16,2048]{2,1,0:T(8,128)(2,1)S(1)} %slice.15), channel_id=1, source_target_pairs={{0,4},{4,8},{8,12},{12,16},{16,20},{20,24},{24,28},{1,5},{5,9},{9,... | collective-permute-start | bytes 589832 | tf_op jit(solution)/shard_map/ppermute | solution.py:26
  86.5 0.0 copy-done.3
  86.5 0.2 reduce-window.15
  86.7 0.0 copy-done.1
  86.8 0.1 select_reduce_fusion
  86.9 2.3 collective-permute-done.refs_4_
  89.1 0.1 broadcast_in_dim.31.refs_6_.back_ref
  89.2 0.0 copy-start.2
  89.2 0.0 copy-start
  89.2 10.4 %short_conv.1 = (f32[256,2048]{1,0:T(8,128)S(1)}, bf16[256,2048]{1,0:T(8,128)(2,1)S(1)}) custom-call(s32[4]{0:T(128)S(1)} %get-tuple-element.9.wanted_ref, bf16[8,3,64,2048]{3,2,1,0:T(8,128)(2,1)} %exchange.1.refs_0_.refs_1_.refs_2_.refs_3_, bf16[8,3,64,2048]{3,2,1,0:T(8,128)(2,1)} %exchange.1.refs_0_.refs_1_.refs_2_.refs_3_, ...), custom_call_target="tpu_custom_call" | custom-call | tf_op jit(solution)/shard_map/short_conv/pallas_call | solution.py:119
  99.7 0.8 slice.12
  100.5 4.4 %collective-permute-start.1 = (bf16[128,2048]{1,0:T(8,128)(2,1)}, bf16[128,2048]{1,0:T(8,128)(2,1)}, u32[]{:S(2)}, u32[]{:S(2)}) collective-permute-start(bf16[128,2048]{1,0:T(8,128)(2,1)} %slice.12), channel_id=1, source_target_pairs={{0,4},{4,8},{8,12},{12,16},{16,20},{20,24},{24,28},{1,5},{5,9},{9,... | collective-permute-start | bytes 1572872 | tf_op jit(solution)/shard_map/ppermute | solution.py:26
  104.9 0.0 copy-done.2
  104.9 0.1 pad.2.clone
  105.0 0.1 maximum_maximum_fusion
  105.1 0.1 copy.9
  105.3 6.0 %collective-permute-done.1.prev_ref = bf16[128,2048]{1,0:T(8,128)(2,1)} collective-permute-done((bf16[128,2048]{1,0:T(8,128)(2,1)}, bf16[128,2048]{1,0:T(8,128)(2,1)}, u32[]{:S(2)}, u32[]{:S(2)}) %collective-permute-start.1) | collective-permute-done | bytes 524320 | tf_op jit(solution)/shard_map/ppermute | solution.py:26
  111.3 0.0 copy-done
  111.3 7.7 %medium_conv.1.hid_ref = bf16[256,2048]{1,0:T(8,128)(2,1)S(1)} custom-call(bf16[128,2048]{1,0:T(8,128)(2,1)} %collective-permute-done.1.prev_ref, bf16[256,2048]{1,0:T(8,128)(2,1)S(1)} %get-tuple-element.7.z_ref, f32[256,2048]{1,0:T(8,128)S(1)} %get-tuple-element.8.q_ref, f32[1,2048]{1,0:T(1,128)S(1)} %bitcast.20, f32[8,16,256]{2,1,0:T(8,128)S(1)} %bitcast.19, ...), custom_call_target="tpu_custom_call" | custom-call | tf_op jit(solution)/shard_map/medium_conv/pallas_call | solution.py:188
  119.0 120.8 %project.1 = bf16[256,2048]{1,0:T(8,128)(2,1)S(1)} custom-call(bf16[256,2048]{1,0:T(8,128)(2,1)S(1)} %medium_conv.1.hid_ref, bf16[2048,1024]{1,0:T(8,128)(2,1)} %w_ref.1), custom_call_target="tpu_custom_call" | custom-call | tf_op jit(solution)/shard_map/project/pallas_call | solution.py:405
  239.8 1.0 copy.11
  (12 shorter events, 0.1 us)
Async XLA Ops:
  10.0 76.6 %copy-start.3 = (s32[8]{0:T(128)S(1)}, s32[8]{0:T(128)}, u32[]{:S(2)}) copy-start(s32[8]{0:T(128)} %param.12) | copy-start | bytes 100
  10.0 76.8 %copy-start.1 = (bf16[3,7,2048]{2,1,0:T(8,128)(2,1)S(1)}, bf16[3,7,2048]{2,1,0:T(8,128)(2,1)}, u32[]{:S(2)}) copy-start(bf16[3,7,2048]{2,1,0:T(8,128)(2,1)} %param.8) | copy-start | bytes 258052
  83.9 5.2 %collective-permute-start = (bf16[3,16,2048]{2,1,0:T(8,128)(2,1)S(1)}, bf16[3,16,2048]{2,1,0:T(8,128)(2,1)S(1)}, u32[]{:S(2)}, u32[]{:S(2)}) collective-permute-start(bf16[3,16,2048]{2,1,0:T(8,128)(2,1)S(1)} %slice.15), channel_id=1, source_target_pairs={{0,4},{4,8},{8,12},{12,16},{16,20},{20,24},{24,28},{1,5},{5,9},{9,... | collective-permute-start | bytes 589832 | tf_op jit(solution)/shard_map/ppermute | solution.py:26
  89.2 15.7 %copy-start.2 = (bf16[128,128]{1,0:T(8,128)(2,1)S(1)}, bf16[128,128]{1,0:T(8,128)(2,1)}, u32[]{:S(2)}) copy-start(bf16[128,128]{1,0:T(8,128)(2,1)} %param.9) | copy-start | bytes 98308
  89.2 22.1 %copy-start = (f32[2048]{0:T(1024)S(1)}, f32[2048]{0:T(1024)}, u32[]{:S(2)}) copy-start(f32[2048]{0:T(1024)} %param.10) | copy-start | bytes 24580
  100.5 10.8 %collective-permute-start.1 = (bf16[128,2048]{1,0:T(8,128)(2,1)}, bf16[128,2048]{1,0:T(8,128)(2,1)}, u32[]{:S(2)}, u32[]{:S(2)}) collective-permute-start(bf16[128,2048]{1,0:T(8,128)(2,1)} %slice.12), channel_id=1, source_target_pairs={{0,4},{4,8},{8,12},{12,16},{16,20},{20,24},{24,28},{1,5},{5,9},{9,... | collective-permute-start | bytes 1572872 | tf_op jit(solution)/shard_map/ppermute | solution.py:26

commit v3 on v2

--- a/solution.py
+++ b/solution.py
@@ -87,7 +87,7 @@
 
     def conv(i, sl):
         ext = jnp.concatenate(
-            [edge_ref[i, :, sl].astype(jnp.float32)]
+            [edge_ref[0, i, :, sl].astype(jnp.float32)]
             + [b[0, i, :, sl].astype(jnp.float32) for b in block_refs],
             axis=0,
         )
@@ -103,25 +103,35 @@
         z_ref[:, sl] = (conv(1, sl) * conv(2, sl)).astype(z_ref.dtype)
 
 
-def short_stage(incoming, wanted, edge, filt, back):
+def short_stage(incoming, wanted, half, edge, filt, back):
     n, _, blk, width = incoming.shape
-    nb = wanted.shape[0]
+    nb = wanted.shape[0] // 2
+    first = half * nb
     rows = nb * blk
     lanes = 256
-    in_specs = [
-        pl.BlockSpec((1, 3, blk, lanes), functools.partial(lambda k, i, w: (w[k], 0, 0, i), k))
-        for k in range(nb)
-    ] + [
-        pl.BlockSpec((3, EDGE, lanes), lambda i, w: (0, 0, i)),
-        pl.BlockSpec((3, filt.shape[1], lanes), lambda i, w: (0, 0, i)),
-        pl.BlockSpec((rows, 128), lambda i, w: (0, 0)),
-    ]
+
+    def block_at(k):
+        return pl.BlockSpec((1, 3, blk, lanes), lambda i, w: (w[first + k], 0, 0, i))
+
+    if edge is None:
+        edge = incoming
+        edge_spec = pl.BlockSpec(
+            (1, 3, EDGE, lanes), lambda i, w: (w[first - 1], 0, blk // EDGE - 1, i)
+        )
+    else:
+        edge_spec = pl.BlockSpec((1, 3, EDGE, lanes), lambda i, w: (0, 0, 0, i))
+    span = filt.shape[1]
     return pl.pallas_call(
         functools.partial(short_kernel, nb),
         grid_spec=pltpu.PrefetchScalarGridSpec(
             num_scalar_prefetch=1,
             grid=(width // lanes,),
-            in_specs=in_specs,
+            in_specs=[block_at(k) for k in range(nb)]
+            + [
+                edge_spec,
+                pl.BlockSpec((3, span, lanes), lambda i, w: (0, 0, i)),
+                pl.BlockSpec((rows, 128), lambda i, w: (half, 0)),
+            ],
             out_specs=[
                 pl.BlockSpec((rows, lanes), lambda i, w: (0, i)),
                 pl.BlockSpec((rows, lanes), lambda i, w: (0, i)),
@@ -132,75 +142,85 @@
             jax.ShapeDtypeStruct((rows, width), jnp.bfloat16),
         ],
         compiler_params=pltpu.CompilerParams(vmem_limit_bytes=48 * 2**20),
+        cost_estimate=pl.CostEstimate(
+            flops=9 * span * rows * width * 8, bytes_accessed=12 * rows * width, transcendentals=0
+        ),
         name="short_conv",
     )(wanted, *([incoming] * nb), edge, filt, back)
 
 
-def medium_kernel(per_group, span, prev_ref, z_ref, q_ref, skip_ref, line_ref, back_ref, h_ref):
-    rows, lanes = z_ref.shape
+def medium_kernel(per_group, span, prev_ref, z_ref, q_ref, skip_ref, line_ref, back_ref, *refs):
+    h_ref = refs[-1]
+    lanes = z_ref.shape[1]
     row = lax.broadcasted_iota(jnp.int32, (span, 2 * span), 0)
     col = lax.broadcasted_iota(jnp.int32, (span, 2 * span), 1)
-    step = span + row - col
     lane = lax.broadcasted_iota(jnp.int32, (span, 128), 1)
-    tiles = rows // span
-    keeps = [
-        step <= jnp.concatenate([back_ref[r * span : (r + 1) * span]] * 2, axis=1)
-        for r in range(tiles)
-    ]
+    keeps = span + row - col <= jnp.concatenate([back_ref[...]] * 2, axis=1)
     groups = 128 // per_group
     for lo in range(0, lanes, 128):
         sl = slice(lo, lo + 128)
         ext = jnp.concatenate([prev_ref[:, sl], z_ref[:, sl]], axis=0)
-        total = [jnp.zeros((span, 128), jnp.float32) for _ in range(tiles)]
+        total = jnp.zeros((span, 128), jnp.float32)
         for g in range(groups):
             line = line_ref[0, lo // per_group + g : lo // per_group + g + 1, :]
             band = pltpu.roll(
                 jnp.broadcast_to(line, (span, 2 * span)), 0, 1, stride=1, stride_axis=0
             )
+            kept = jnp.where(keeps, band, 0.0).astype(jnp.bfloat16)
+            part = jnp.dot(kept, ext, preferred_element_type=jnp.float32)
             mine = (lane >= g * per_group) & (lane < (g + 1) * per_group)
-            for r in range(tiles):
-                kept = jnp.where(keeps[r], band, 0.0).astype(jnp.bfloat16)
-                part = jnp.dot(
-                    kept,
-                    ext[r * span : (r + 2) * span],
-                    preferred_element_type=jnp.float32,
-                )
-                total[r] = jnp.where(mine, part, total[r])
-        for r in range(tiles):
-            rs = slice(r * span, (r + 1) * span)
-            full = total[r] + skip_ref[0:1, sl] * z_ref[rs, sl].astype(jnp.float32)
-            h_ref[rs, sl] = (q_ref[rs, sl] * full).astype(h_ref.dtype)
-
-
-def medium_stage(z_prev, z_vals, query, skip, taps, back):
-    rows, width = z_vals.shape
+            total = jnp.where(mine, part, total)
+        full = total + skip_ref[0:1, sl] * z_ref[:, sl].astype(jnp.float32)
+        h_ref[:, sl] = (q_ref[:, sl] * full).astype(h_ref.dtype)
+
+
+def filter_lines(taps):
     span, groups = taps.shape
-    per_group = width // groups
-    lanes = 256
-    line = jnp.concatenate(
+    return jnp.concatenate(
         [
             jnp.zeros((groups, 1), jnp.float32),
             jnp.transpose(taps[::-1]).astype(jnp.float32),
             jnp.zeros((groups, span - 1), jnp.float32),
         ],
         axis=1,
-    ).reshape(width // lanes, lanes // per_group, 2 * span)
+    )
+
+
+def medium_stage(z_prev, z_vals, query, skip, taps, back, half, into):
+    span, width = z_vals.shape
+    groups = taps.shape[1]
+    per_group = width // groups
+    lanes = 256
+    line = filter_lines(taps).reshape(width // lanes, lanes // per_group, 2 * span)
+    in_specs = [
+        pl.BlockSpec((span, lanes), lambda i: (0, i)),
+        pl.BlockSpec((span, lanes), lambda i: (0, i)),
+        pl.BlockSpec((span, lanes), lambda i: (0, i)),
+        pl.BlockSpec((1, lanes), lambda i: (0, i)),
+        pl.BlockSpec((1, lanes // per_group, 2 * span), lambda i: (i, 0, 0)),
+        pl.BlockSpec((span, 128), lambda i: (half, 0)),
+    ]
+    args = [z_prev, z_vals, query, skip, line, back]
+    aliases = {}
+    if into is not None:
+        aliases = {len(args): 0}
+        args.append(into)
+        in_specs.append(pl.BlockSpec(memory_space=pl.ANY))
     return pl.pallas_call(
         functools.partial(medium_kernel, per_group, span),
         grid=(width // lanes,),
-        in_specs=[
-            pl.BlockSpec((span, lanes), lambda i: (0, i)),
-            pl.BlockSpec((rows, lanes), lambda i: (0, i)),
-            pl.BlockSpec((rows, lanes), lambda i: (0, i)),
-            pl.BlockSpec((1, lanes), lambda i: (0, i)),
-            pl.BlockSpec((1, lanes // per_group, 2 * span), lambda i: (i, 0, 0)),
-            pl.BlockSpec((rows, 128), lambda i: (0, 0)),
-        ],
-        out_specs=pl.BlockSpec((rows, lanes), lambda i: (0, i)),
-        out_shape=jax.ShapeDtypeStruct((rows, width), jnp.bfloat16),
+        in_specs=in_specs,
+        out_specs=pl.BlockSpec((span, lanes), lambda i: (half, i)),
+        out_shape=jax.ShapeDtypeStruct((2 * span, width), jnp.bfloat16),
+        input_output_aliases=aliases,
         compiler_params=pltpu.CompilerParams(vmem_limit_bytes=48 * 2**20),
+        cost_estimate=pl.CostEstimate(
+            flops=2 * groups * span * 2 * span * 256,
+            bytes_accessed=10 * span * width,
+            transcendentals=0,
+        ),
         name="medium_conv",
-    )(z_prev, z_vals, query, skip, line, back)
+    )(*args)
 
 
 def project_kernel(
@@ -449,7 +469,6 @@
     blk = source_rows.shape[0] // stretches
     rows = nb_own * blk
     width = source_rows.shape[2]
-    mr_len = medium_filters.shape[0]
     member = jnp.any(block_packing_device == me, axis=1)
     flags = member.astype(jnp.int32)
     slots = jnp.minimum(jnp.cumsum(flags) - flags, stretches - 1)
@@ -464,11 +483,15 @@
     begin = jnp.max(jnp.where(starts[None, :] <= positions[:, None], starts[None, :], 0), axis=1)
     back = jnp.broadcast_to((positions - begin)[:, None], (rows, 128))
 
-    last = lax.dynamic_index_in_dim(incoming, wanted[nb_own - 1], 0, keepdims=False)
-    edge = passed_along(last[:, blk - EDGE :], "ctx", 1)
-    query, z_vals = short_stage(incoming, wanted, edge, short_filters.astype(jnp.float32), back)
-    z_prev = passed_along(z_vals[rows - mr_len :], "ctx", 1)
-    hidden = medium_stage(z_prev, z_vals, query, skip_gain[None, :], medium_filters, back)
+    last = lax.dynamic_index_in_dim(incoming, wanted[nb_own - 1], 0, keepdims=True)
+    edge = passed_along(last[:, :, blk - EDGE :], "ctx", 1)
+    taps = short_filters.astype(jnp.float32)
+    skip = skip_gain[None, :]
+    q_late, z_late = short_stage(incoming, wanted, 1, None, taps, back)
+    z_prev = passed_along(z_late, "ctx", 1)
+    q_early, z_early = short_stage(incoming, wanted, 0, edge, taps, back)
+    hidden = medium_stage(z_early, z_late, q_late, skip, medium_filters, back, 1, None)
+    hidden = medium_stage(z_prev, z_early, q_early, skip, medium_filters, back, 0, hidden)
     return project(hidden, out_weight)
 
 

time: 242 us -> 234 us (0.967)
  waiting for transfers between devices: 8.31 us -> 0.01 us
  Pallas kernels: 211 us -> 214 us
  starting transfers between devices: 6.95 us -> 4.49 us
    ppermute x2, waiting for transfers between devices: 8.31 us -> 0.01 us  [passed_along(): return lax.ppermute(block, axis, route)]
    pallas_call x1 -> x2, Pallas kernels: 10.4 us -> 14.1 us  [short_stage(): pl.pallas_call(functools.partial(short_kernel, nb), grid_spec=pltpu.Prefe...]
    pallas_call x1, Pallas kernels: 121 us -> 118 us  [project(): pl.pallas_call(functools.partial(project_kernel, n, m), out_shape=jax.Sha...]
    ppermute x2, starting transfers between devices: 6.95 us -> 4.49 us  [passed_along(): return lax.ppermute(block, axis, route)]
    pallas_call x1 -> x2, Pallas kernels: 7.69 us -> 9.43 us  [medium_stage(): pl.pallas_call(functools.partial(medium_kernel, per_group, span), grid=(w...]
  transfers between devices with their start and end apart: 2 -> 2, of which waited for: 2 -> 0; matrix products, arithmetic and copies ran while one was open for 0% -> 0% of each run, Pallas kernels for 0% -> 8%
where the time goes in v3:
time: 234 us; the launch traced here: 232 us
  Pallas kernels  214 us (91%)
  local copies, waits for them, and re-layouts  10 us (4%)
  starting transfers between devices  4.49 us (2%)
    pallas_call x1, Pallas kernels, project(): pl.pallas_call(functools.partial(project_kernel, n, m), out_shape=jax.Sha...  118 us
    pallas_call x1, Pallas kernels, exchange(): pl.pallas_call(functools.partial(exchange_kernel, n), out_shape=jax.Shape...  72.1 us
    pallas_call x2, Pallas kernels, short_stage(): pl.pallas_call(functools.partial(short_kernel, nb), grid_spec=pltpu.Prefe...  14.1 us
    pallas_call x2, Pallas kernels, medium_stage(): pl.pallas_call(functools.partial(medium_kernel, per_group, span), grid=(w...  9.43 us
    gather x1, local copies, waits for them, and re-layouts, on_device(): jnp.take(blocks, slots, axis=0, mode='clip').transpose(0, 2, 1, 3)  6.39 us
  transfers between devices with their start and end apart: 2, of which 0 were waited for; matrix products, arithmetic and copies ran while one was open for 0% of the time, Pallas kernels for 8%

profile of v3, /device:TPU:13, one launch (start us, length us, event | category | flops | bytes accessed | tf_op | source)
XLA Modules:
  0.0 231.5 jit_solution(13334202382776968231)
XLA Ops:
  0.0 0.9 fusion.1
  0.9 0.5 slice.7
  2.7 0.7 compare_reduce_fusion
  3.4 0.2 reduce-window.14
  3.6 6.4 %gather_fusion = bf16[8,64,3,2048]{3,1,2,0:T(8,128)(2,1)} fusion(bf16[8,64,3,2048]{3,1,0,2:T(8,128)(2,1)} %bitcast.22, s32[1024]{0:T(1024)S(1)} %pad_clamp_fusion), kind=kCustom, calls=%fused_computation | custom fusion | bytes 12582944 | tf_op jit(solution)/shard_map/jit(_take)/gather | solution.py:476
  10.0 0.0 copy-start.3
  10.0 0.0 copy-start.1
  10.0 72.1 %exchange.1.refs_0_.refs_1_.refs_2_ = bf16[8,3,64,2048]{3,2,1,0:T(8,128)(2,1)} custom-call(bf16[8,3,64,2048]{3,2,1,0:T(8,128)(2,1)} %bitcast.21), custom_call_target="tpu_custom_call" | custom-call | tf_op jit(solution)/shard_map/exchange/pallas_call | solution.py:66
  82.7 1.0 constant_dynamic-slice_fusion
  83.7 2.6 %collective-permute-start.1 = (bf16[1,3,16,2048]{3,2,1,0:T(8,128)(2,1)S(1)}, bf16[1,3,16,2048]{3,2,1,0:T(8,128)(2,1)S(1)}, u32[]{:S(2)}, u32[]{:S(2)}) collective-permute-start(bf16[1,3,16,2048]{3,2,1,0:T(8,128)(2,1)S(1)} %constant_dynamic-slice_fusion), channel_id=1, source_target_pairs={{0,4},{4,8},{8,12},{12,16},{16,20},{20,24},{24,28},{1,5},{5,9},{9,... | collective-permute-start | bytes 589832 | tf_op jit(solution)/shard_map/ppermute | solution.py:26
  86.3 0.0 copy-done.3
  86.3 0.2 reduce-window.15
  86.5 0.1 select_reduce_fusion
  86.6 0.0 copy-done.1
  86.6 0.1 broadcast_in_dim.17.refs_4_.back_ref
  86.7 0.0 copy-start.2
  86.7 7.1 %short_conv.2 = (f32[128,2048]{1,0:T(8,128)S(1)}, bf16[128,2048]{1,0:T(8,128)(2,1)S(1)}) custom-call(s32[4]{0:T(128)S(1)} %get-tuple-element.13.wanted_ref, bf16[8,3,64,2048]{3,2,1,0:T(8,128)(2,1)} %exchange.1.refs_0_.refs_1_.refs_2_, bf16[8,3,64,2048]{3,2,1,0:T(8,128)(2,1)} %exchange.1.refs_0_.refs_1_.refs_2_, ...), custom_call_target="tpu_custom_call" | custom-call | flops 132120576 | bytes 3145728 | tf_op jit(solution)/shard_map/short_conv/pallas_call | solution.py:124
  93.8 1.9 collective-permute-start
  95.7 0.0 copy-done.2
  95.8 0.1 pad.2.clone
  95.9 0.1 maximum_maximum_fusion
  96.0 0.1 copy.10
  96.1 0.0 copy-start
  96.1 0.0 collective-permute-done.1.refs_2_
  96.1 7.0 %short_conv.3 = (f32[128,2048]{1,0:T(8,128)S(1)}, bf16[128,2048]{1,0:T(8,128)(2,1)S(1)}) custom-call(s32[4]{0:T(128)S(1)} %get-tuple-element.13.wanted_ref, bf16[8,3,64,2048]{3,2,1,0:T(8,128)(2,1)} %exchange.1.refs_0_.refs_1_.refs_2_, bf16[8,3,64,2048]{3,2,1,0:T(8,128)(2,1)} %exchange.1.refs_0_.refs_1_.refs_2_, ...), custom_call_target="tpu_custom_call" | custom-call | flops 132120576 | bytes 3145728 | tf_op jit(solution)/shard_map/short_conv/pallas_call | solution.py:124
  103.2 0.0 copy-done
  103.2 4.7 %medium_conv.2.refs_0_ = bf16[256,2048]{1,0:T(8,128)(2,1)S(1)} custom-call(bf16[128,2048]{1,0:T(8,128)(2,1)S(1)} %get-tuple-element.10.prev_ref.z_ref, bf16[128,2048]{1,0:T(8,128)(2,1)S(1)} %get-tuple-element.9.z_ref, f32[128,2048]{1,0:T(8,128)S(1)} %get-tuple-element.12.q_ref, f32[1,2048]{1,0:T(1,128)S(1)} %bitcast.19, f32[8,16,256]{2,1,0:T(8,128)S(1)} %bitcast.17, ...), custom_call_target="tpu_custom_call" | custom-call | flops 2147483648 | bytes 2621440 | tf_op jit(solution)/shard_map/medium_conv/pallas_call | solution.py:209
  107.9 0.0 collective-permute-done.prev_ref
  107.9 4.7 %medium_conv.3.hid_ref = bf16[256,2048]{1,0:T(8,128)(2,1)S(1)} custom-call(bf16[128,2048]{1,0:T(8,128)(2,1)S(1)} %collective-permute-done.prev_ref, bf16[128,2048]{1,0:T(8,128)(2,1)S(1)} %get-tuple-element.10.prev_ref.z_ref, f32[128,2048]{1,0:T(8,128)S(1)} %get-tuple-element.11.q_ref, f32[1,2048]{1,0:T(1,128)S(1)} %bitcast.20, ...), custom_call_target="tpu_custom_call", output_to_operand_aliasing={{}: (6, {})} | custom-call | flops 2147483648 | bytes 2621440 | tf_op jit(solution)/shard_map/medium_conv/pallas_call | solution.py:209
  112.6 117.9 %project.1 = bf16[256,2048]{1,0:T(8,128)(2,1)S(1)} custom-call(bf16[256,2048]{1,0:T(8,128)(2,1)S(1)} %medium_conv.3.hid_ref, bf16[2048,1024]{1,0:T(8,128)(2,1)} %w_ref.1), custom_call_target="tpu_custom_call" | custom-call | tf_op jit(solution)/shard_map/project/pallas_call | solution.py:425
  230.5 1.0 copy.13
  (11 shorter events, 0.1 us)
Async XLA Ops:
  10.0 76.3 %copy-start.3 = (s32[8]{0:T(128)S(1)}, s32[8]{0:T(128)}, u32[]{:S(2)}) copy-start(s32[8]{0:T(128)} %param.12) | copy-start | bytes 100
  10.0 76.6 %copy-start.1 = (bf16[3,7,2048]{2,1,0:T(8,128)(2,1)S(1)}, bf16[3,7,2048]{2,1,0:T(8,128)(2,1)}, u32[]{:S(2)}) copy-start(bf16[3,7,2048]{2,1,0:T(8,128)(2,1)} %param.8) | copy-start | bytes 258052
  83.7 12.4 %collective-permute-start.1 = (bf16[1,3,16,2048]{3,2,1,0:T(8,128)(2,1)S(1)}, bf16[1,3,16,2048]{3,2,1,0:T(8,128)(2,1)S(1)}, u32[]{:S(2)}, u32[]{:S(2)}) collective-permute-start(bf16[1,3,16,2048]{3,2,1,0:T(8,128)(2,1)S(1)} %constant_dynamic-slice_fusion), channel_id=1, source_target_pairs={{0,4},{4,8},{8,12},{12,16},{16,20},{20,24},{24,28},{1,5},{5,9},{9,... | collective-permute-start | bytes 589832 | tf_op jit(solution)/shard_map/ppermute | solution.py:26
  86.7 9.0 %copy-start.2 = (bf16[128,128]{1,0:T(8,128)(2,1)S(1)}, bf16[128,128]{1,0:T(8,128)(2,1)}, u32[]{:S(2)}) copy-start(bf16[128,128]{1,0:T(8,128)(2,1)} %param.9) | copy-start | bytes 98308
  93.8 14.1 %collective-permute-start = (bf16[128,2048]{1,0:T(8,128)(2,1)S(1)}, bf16[128,2048]{1,0:T(8,128)(2,1)S(1)}, u32[]{:S(2)}, u32[]{:S(2)}) collective-permute-start(bf16[128,2048]{1,0:T(8,128)(2,1)S(1)} %get-tuple-element.9.z_ref), channel_id=1, source_target_pairs={{0,4},{4,8},{8,12},{12,16},{16,20},{20,24},{24,28},{1,5},{5,9},{9,... | collective-permute-start | bytes 1572872 | tf_op jit(solution)/shard_map/ppermute | solution.py:26
  96.1 7.1 %copy-start = (f32[2048]{0:T(1024)S(1)}, f32[2048]{0:T(1024)}, u32[]{:S(2)}) copy-start(f32[2048]{0:T(1024)} %param.10) | copy-start | bytes 24580
